TPU v7x, 32 devices: a whole 2x2x4 slice. The times are simulated.
32 devices in a mesh: dp: 16 (over z, y, core), tensor: 2 (over x).
Axes of the slice: x: 2, y: 2, z: 4, core: 2. Of those that a mesh axis runs over, the one named last changes fastest.
Arguments:
- tokens: bfloat16 [6144, 4096], P(('dp', 'tensor')), may hold values from -21 to 21
- wq_codes: bfloat16 [4096, 1024], P('dp', 'tensor'), may hold values from -4 to 4
- wq_scales: float32 [32, 8], replicated, may hold values from 0.0078125 to 0.03125
- wk_codes: bfloat16 [4096, 128], P('dp', 'tensor'), may hold values from -4 to 4
- wk_scales: float32 [32, 1], replicated, may hold values from 0.0078125 to 0.03125
- wv_codes: bfloat16 [4096, 128], P('dp', 'tensor'), may hold values from -4 to 4
- wv_scales: float32 [32, 1], replicated, may hold values from 0.0078125 to 0.03125
- wo_codes: bfloat16 [1024, 4096], P('tensor', 'dp'), may hold values from -4 to 4
- wo_scales: float32 [8, 32], replicated, may hold values from 0.015625 to 0.0625
Outputs:
- mixed: bfloat16 [6144, 4096], P(('dp', 'tensor'))
All inputs are finite; a program needn't handle non-finite values.
Results may differ from a plain program's by a relative error of at most 0.014.
The roundings to bfloat16 on the way count: a program that leaves them out, or rounds other values in their place, can miss the bound.
Values may be sent and summed in bfloat16 or wider, within the bound.
A program may use at most 64 MiB of HBM per device.

v0:
```python
import jax
import jax.numpy as jnp
from jax import lax
from jax.sharding import PartitionSpec as P

HEAD = 128
BLOCK = 128
SPAN = 384
rope_base = 500000.0
masked_value = -1e30


def from_partner(value, axis, apart):
    mask = 2**apart
    pairs = [(source, source ^ mask) for source in range(lax.axis_size(axis))]
    return lax.ppermute(value, axis, pairs)


def dequantize(codes, scales, row_start, col_start):
    height, breadth = codes.shape
    row_block = (row_start + jnp.arange(height, dtype=jnp.int32)) // BLOCK
    col_block = (col_start + jnp.arange(breadth, dtype=jnp.int32)) // BLOCK
    row_pick = (row_block[:, None] == jnp.arange(scales.shape[0], dtype=jnp.int32)[None, :]).astype(
        jnp.float32
    )
    col_pick = (col_block[None, :] == jnp.arange(scales.shape[1], dtype=jnp.int32)[:, None]).astype(
        jnp.float32
    )
    picked = jnp.dot(row_pick, scales, precision=lax.Precision.HIGHEST)
    expanded = jnp.dot(picked, col_pick, precision=lax.Precision.HIGHEST)
    return (codes.astype(jnp.float32) * expanded).astype(jnp.bfloat16)


def rotate(features, positions):
    half_size = HEAD // 2
    steps = jnp.arange(half_size).astype(jnp.float32)
    inverse = jnp.exp(-(2.0 * steps / HEAD) * jnp.log(jnp.float32(rope_base)))
    angle = positions[:, None] * inverse[None, :]
    cosine = jnp.cos(angle)[:, None, :]
    sine = jnp.sin(angle)[:, None, :]
    first = features[..., :half_size]
    second = features[..., half_size:]
    return jnp.concatenate(
        [first * cosine - second * sine, second * cosine + first * sine], axis=-1
    )


def in_order(upper, mine, partner):
    return jnp.where(
        upper, jnp.concatenate([partner, mine], axis=1), jnp.concatenate([mine, partner], axis=1)
    )


def body(
    tokens, wq_codes, wq_scales, wk_codes, wk_scales, wv_codes, wv_scales, wo_codes, wo_scales
):
    data_index = lax.axis_index("dp")
    head_index = lax.axis_index("tensor")
    weight_rows = wq_codes.shape[0]
    row_start = data_index * weight_rows
    query_width = wq_codes.shape[1]
    shard_width = wk_codes.shape[1]
    wq_local = dequantize(wq_codes, wq_scales, row_start, head_index * query_width)
    wk_local = dequantize(wk_codes, wk_scales, row_start, head_index * shard_width)
    wv_local = dequantize(wv_codes, wv_scales, row_start, head_index * shard_width)
    wo_local = dequantize(
        wo_codes, wo_scales, head_index * wo_codes.shape[0], data_index * wo_codes.shape[1]
    )
    wo_whole = lax.all_gather(wo_local, "dp", axis=1, tiled=True)
    sequence = lax.all_gather(tokens, "tensor", axis=0, tiled=True)
    upper = head_index % 2 == 1
    partner_k, partner_v = from_partner((wk_local, wv_local), "tensor", 0)
    wk_used = in_order(upper, wk_local, partner_k)
    wv_used = in_order(upper, wv_local, partner_v)
    length = sequence.shape[0]
    full_q, full_k, full_v = (
        lax.all_gather(wq_local, "dp", axis=0, tiled=True),
        lax.all_gather(wk_used, "dp", axis=0, tiled=True),
        lax.all_gather(wv_used, "dp", axis=0, tiled=True),
    )
    query_lin = jnp.dot(sequence, full_q, preferred_element_type=jnp.float32)
    key_lin = jnp.dot(sequence, full_k, preferred_element_type=jnp.float32)
    value_lin = jnp.dot(sequence, full_v, preferred_element_type=jnp.float32)
    positions = (jnp.arange(length) % SPAN).astype(jnp.float32)
    heads_here = query_width // HEAD
    span_count = length // SPAN
    queries = rotate(query_lin.reshape(length, heads_here, HEAD), positions).astype(jnp.bfloat16)
    keys = rotate(key_lin.reshape(length, 1, HEAD), positions)[:, 0, :].astype(jnp.bfloat16)
    values = value_lin.astype(jnp.bfloat16)
    queries = queries.reshape(span_count, SPAN, heads_here, HEAD)
    keys = keys.reshape(span_count, SPAN, HEAD)
    values = values.reshape(span_count, SPAN, HEAD)
    causal = jnp.arange(SPAN)[:, None] >= jnp.arange(SPAN)[None, :]
    scores = jnp.einsum("cqhd,ckd->chqk", queries, keys, preferred_element_type=jnp.float32) * (
        1.0 / HEAD**0.5
    )
    scores = jnp.where(causal[None, None, :, :], scores, masked_value)
    peak = jnp.max(scores, axis=-1, keepdims=True)
    powers = jnp.exp(scores - peak)
    total = jnp.sum(powers, axis=-1, keepdims=True)
    probs = (powers / total).astype(jnp.bfloat16)
    attended = (
        jnp.einsum("chqk,ckd->cqhd", probs, values, preferred_element_type=jnp.float32)
        .astype(jnp.bfloat16)
        .reshape(length, query_width)
    )
    terms = jnp.dot(attended, wo_whole, preferred_element_type=jnp.float32)
    mixed = lax.psum_scatter(terms.astype(jnp.bfloat16), "tensor", scatter_dimension=0, tiled=True)
    return mixed


def solution(mesh):
    return jax.shard_map(
        body,
        mesh=mesh,
        in_specs=(
            P(("dp", "tensor"), None),
            P("dp", "tensor"),
            P(),
            P("dp", "tensor"),
            P(),
            P("dp", "tensor"),
            P(),
            P("tensor", "dp"),
            P(),
        ),
        out_specs=P(("dp", "tensor"), None),
        check_vma=False,
    )
```

profile of v0, /device:TPU:0, one launch (start us, length us, event | category | flops | bytes accessed | tf_op | source)
XLA Modules:
  0.0 298.7 jit_solution(14492165854905876810)
XLA Ops:
  6.6 0.9 fusion.18
  7.5 0.9 fusion.17
  8.4 0.9 multiply_convert_fusion.1
  9.3 3.0 %collective-permute-start.1 = (bf16[256,64]{0,1:T(8,128)(2,1)S(1)}, bf16[256,64]{0,1:T(8,128)(2,1)S(1)}, u32[]{:S(2)}, u32[]{:S(2)}) collective-permute-start(bf16[256,64]{0,1:T(8,128)(2,1)S(1)} %get-tuple-element.14), channel_id=1, source_target_pairs={{0,1},{1,0},{2,3},{3,2},{4,5},{5,4},{6,7},{7,6},{8,9},{9,8},{10,11... | collective-permute-start | bytes 98312 | tf_op jit(solution)/shard_map/ppermute | solution.py:16
  12.3 1.9 collective-permute-done.1
  14.9 0.7 all-gather.8.cloned.1.call-update
  15.7 0.9 fusion.16
  16.7 1.1 fusion.2
  17.8 2.1 collective-permute-start
  19.9 1.9 collective-permute-done
  22.8 1.1 fusion.3
  24.1 1.4 multiply_cosine_fusion
  25.5 28.1 %all-gather.10.cloned.1.call-done = bf16[4096,128]{0,1:T(8,128)(2,1)} async-done(((bf16[256,128]{0,1:T(8,128)(2,1)}), bf16[4096,128]{0,1:T(8,128)(2,1)}) %all-gather.10.cloned.1.call-update) | async-done | bytes 1048592 | tf_op jit(solution)/shard_map/all_gather | solution.py:78
  53.6 46.0 %all-gather.8.cloned.1.call-done = bf16[384,4096]{1,0:T(8,128)(2,1)} async-done(((bf16[192,4096]{1,0:T(8,128)(2,1)}), bf16[384,4096]{1,0:T(8,128)(2,1)}) %all-gather.8.cloned.1.call-update) | async-done | bytes 3145744 | tf_op jit(solution)/shard_map/all_gather | solution.py:70
  99.6 3.4 %convolution_bitcast_fusion = f32[384,1,128]{0,2,1:T(8,128)S(1)} fusion(bf16[4096,128]{0,1:T(8,128)(2,1)} %all-gather.10.cloned.1.call-done, bf16[384,4096]{1,0:T(8,128)(2,1)} %all-gather.8.cloned.1.call-done), kind=kOutput, calls=%fused_computation.12 | convolution fusion | flops 402653184 | bytes 4390912 | tf_op jit(solution)/shard_map/dot_general | solution.py:82
  103.1 1.1 fusion.20
  104.1 48.3 %all-gather.12.cloned.1.call-done = bf16[4096,512]{1,0:T(8,128)(2,1)} async-done(((bf16[256,512]{1,0:T(8,128)(2,1)}), bf16[4096,512]{1,0:T(8,128)(2,1)}) %all-gather.12.cloned.1.call-update) | async-done | bytes 4194320 | tf_op jit(solution)/shard_map/all_gather | solution.py:77
  152.4 4.6 %fusion.37 = f32[512,384]{1,0:T(8,128)S(1)} fusion(bf16[4096,512]{1,0:T(8,128)(2,1)} %all-gather.12.cloned.1.call-done, bf16[384,4096]{1,0:T(8,128)(2,1)S(1)} %copy-done.1), kind=kOutput, calls=%fused_computation.79 | convolution fusion | flops 1610612736 | bytes 8126464 | tf_op jit(solution)/shard_map/dot_general | solution.py:81
  158.2 0.7 fusion.1
  159.4 30.4 %all-gather.6.cloned.1.call-done = bf16[4096,128]{0,1:T(8,128)(2,1)} async-done(((bf16[256,128]{0,1:T(8,128)(2,1)}), bf16[4096,128]{0,1:T(8,128)(2,1)}) %all-gather.6.cloned.1.call-update) | async-done | bytes 1048592 | tf_op jit(solution)/shard_map/all_gather | solution.py:79
  189.7 4.1 %convolution_convert_fusion.1 = bf16[128,4,384]{2,0,1:T(8,128)(2,1)S(1)} fusion(f32[384,384,4]{1,0,2:T(8,128)S(1)} %get-tuple-element.16, f32[4,384]{1,0:T(4,128)S(1)} %fusion, f32[4,384]{1,0:T(4,128)S(1)} %get-tuple-element.15, pred[384,384]{0,1:T(8,128)(4,1)S(1)} %iota_compare_fusion, bf16[4096,128]{0,1:T(8,128)(2,1)} %all-gather.6.cloned.1.call-done, ...), kind=kOutput, calls=%fused_computation.6 | convolution fusion | flops 556843008 | bytes 7106560 | tf_op jit(solution)/shard_map/chqk,ckd->cqhd/dot_general | solution.py:103
  193.8 50.7 %all-gather.14.cloned.1.call-done = bf16[512,4096]{1,0:T(8,128)(2,1)} async-done(((bf16[512,256]{1,0:T(8,128)(2,1)}), bf16[512,4096]{1,0:T(8,128)(2,1)}) %all-gather.14.cloned.1.call-update) | async-done | bytes 4194320 | tf_op jit(solution)/shard_map/all_gather | solution.py:69
  244.5 5.7 %convolution_convert_fusion = bf16[384,4096]{1,0:T(8,128)(2,1)} fusion(bf16[384,512]{0,1:T(8,128)(2,1)S(1)} %bitcast.58, bf16[512,4096]{1,0:T(8,128)(2,1)} %all-gather.14.cloned.1.call-done), kind=kOutput, calls=%fused_computation | convolution fusion | flops 1612185600 | bytes 7733248 | tf_op jit(solution)/shard_map/dot_general | solution.py:107
  250.2 41.7 %reduce-scatter.2.cloned.1.call-done = bf16[192,4096]{1,0:T(8,128)(2,1)} async-done(((bf16[384,4096]{1,0:T(8,128)(2,1)}), bf16[192,4096]{1,0:T(8,128)(2,1)}) %reduce-scatter.2.cloned.1.call-update) | async-done | bytes 1572880 | tf_op jit(solution)/shard_map/reduce_scatter | solution.py:108
  (37 shorter events, 3.6 us)
Async XLA Ops:
  6.5 16.0 %copy-start = (f32[8,32]{1,0:T(8,128)S(1)}, f32[8,32]{1,0:T(8,128)}, u32[]{:S(2)}) copy-start(f32[8,32]{1,0:T(8,128)} %param.17) | copy-start | bytes 3076
  6.5 10.1 %copy-start.3 = (bf16[256,512]{1,0:T(8,128)(2,1)S(1)}, bf16[256,512]{1,0:T(8,128)(2,1)}, u32[]{:S(2)}) copy-start(bf16[256,512]{1,0:T(8,128)(2,1)} %param.10) | copy-start | bytes 786436
  6.5 16.3 %copy-start.4 = (bf16[512,256]{1,0:T(8,128)(2,1)S(1)}, bf16[512,256]{1,0:T(8,128)(2,1)}, u32[]{:S(2)}) copy-start(bf16[512,256]{1,0:T(8,128)(2,1)} %param.16) | copy-start | bytes 786436
  6.5 47.1 %all-gather.10.cloned.1.call-start = ((), (), s32[]{:S(2)}) async-start(), calls=%async_computation.3 | async-start | bytes 1114112 | tf_op jit(solution)/shard_map/all_gather | solution.py:78
  9.3 4.9 %collective-permute-start.1 = (bf16[256,64]{0,1:T(8,128)(2,1)S(1)}, bf16[256,64]{0,1:T(8,128)(2,1)S(1)}, u32[]{:S(2)}, u32[]{:S(2)}) collective-permute-start(bf16[256,64]{0,1:T(8,128)(2,1)S(1)} %get-tuple-element.14), channel_id=1, source_target_pairs={{0,1},{1,0},{2,3},{3,2},{4,5},{5,4},{6,7},{7,6},{8,9},{9,8},{10,11... | collective-permute-start | bytes 98312 | tf_op jit(solution)/shard_map/ppermute | solution.py:16
  14.9 84.7 %all-gather.8.cloned.1.call-start = ((), (), s32[]{:S(2)}) async-start(), calls=%async_computation.2 | async-start | bytes 4718592 | tf_op jit(solution)/shard_map/all_gather | solution.py:70
  15.6 136.8 %all-gather.12.cloned.1.call-start = ((), (), s32[]{:S(2)}) async-start(), calls=%async_computation.4 | async-start | bytes 4456448 | tf_op jit(solution)/shard_map/all_gather | solution.py:77
  17.8 172.0 %all-gather.6.cloned.1.call-start = ((), (), s32[]{:S(2)}) async-start(), calls=%async_computation.1 | async-start | bytes 1114112 | tf_op jit(solution)/shard_map/all_gather | solution.py:79
  17.8 4.0 %collective-permute-start = (bf16[256,64]{0,1:T(8,128)(2,1)S(1)}, bf16[256,64]{0,1:T(8,128)(2,1)S(1)}, u32[]{:S(2)}, u32[]{:S(2)}) collective-permute-start(bf16[256,64]{0,1:T(8,128)(2,1)S(1)} %get-tuple-element.13), channel_id=1, source_target_pairs={{0,1},{1,0},{2,3},{3,2},{4,5},{5,4},{6,7},{7,6},{8,9},{9,8},{10,11... | collective-permute-start | bytes 98312 | tf_op jit(solution)/shard_map/ppermute | solution.py:16
  22.4 222.0 %all-gather.14.cloned.1.call-start = ((), (), s32[]{:S(2)}) async-start(), calls=%async_computation.5 | async-start | bytes 4456448 | tf_op jit(solution)/shard_map/all_gather | solution.py:69
  23.9 267.9 %reduce-scatter.2.cloned.1.call-start = ((), (), s32[]{:S(2)}) async-start(), calls=%async_computation.6 | async-start | bytes 4718592 | tf_op jit(solution)/shard_map/reduce_scatter | solution.py:108
  99.6 52.8 %copy-start.1 = (bf16[384,4096]{1,0:T(8,128)(2,1)S(1)}, bf16[384,4096]{1,0:T(8,128)(2,1)}, u32[]{:S(2)}) copy-start(bf16[384,4096]{1,0:T(8,128)(2,1)} %all-gather.8.cloned.1.call-done) | copy-start | bytes 9437188
  157.0 0.9 copy-start.2
  157.1 1.1 copy-start.5
Sparse Core Ops, SparseCore 0:
  15.0 38.5 all-gather.9
  55.2 44.4 all-gather.7
  101.8 50.5 all-gather.11
  154.4 35.2 all-gather.5
  191.7 52.6 all-gather.13
  250.3 41.4 reduce-scatter.1
where the time goes:
time: 299 us
  waiting for transfers between devices  250 us (84%)
  matrix products  23.7 us (8%)
  between operations  13.7 us (5%)
  other arithmetic  5.51 us (2%)
  starting transfers between devices  5.3 us (2%)
    all_gather x1, waiting for transfers between devices, body(): wo_whole = lax.all_gather(wo_local, 'dp', axis=1, tiled=True)  50.7 us
    all_gather x1, waiting for transfers between devices, body(): lax.all_gather(wq_local, 'dp', axis=0, tiled=True)  48.3 us
    all_gather x1, waiting for transfers between devices, body(): sequence = lax.all_gather(tokens, 'tensor', axis=0, tiled=True)  46 us
    reduce_scatter x1, waiting for transfers between devices, body(): lax.psum_scatter(terms.astype(jnp.bfloat16), 'tensor', scatter_dimension=...  41.7 us
    all_gather x1, waiting for transfers between devices, body(): lax.all_gather(wv_used, 'dp', axis=0, tiled=True)  30.4 us
    all_gather x1, waiting for transfers between devices, body(): lax.all_gather(wk_used, 'dp', axis=0, tiled=True)  28.1 us
  transfers between devices with their start and end apart: 8, of which 8 were waited for; matrix products, arithmetic and copies ran while one was open for 7% of the time, Pallas kernels for 0%

commit v1 on v0

--- a/solution.py
+++ b/solution.py
@@ -8,6 +8,12 @@
 SPAN = 384
 rope_base = 500000.0
 masked_value = -1e30
+
+
+def bind_the_records(tile_in, d0):
+    tile_in = jnp.moveaxis(tile_in, 0, d0)
+    met_up = tile_in.shape
+    return tile_in.reshape(*met_up[:d0], met_up[d0] * met_up[d0 + 1], *met_up[d0 + 2 :])
 
 
 def from_partner(value, axis, apart):
@@ -54,6 +60,23 @@
 def body(
     tokens, wq_codes, wq_scales, wk_codes, wk_scales, wv_codes, wv_scales, wo_codes, wo_scales
 ):
+
+    def replace_cards_all(mesh_name, where_dim, content):
+        sides = lax.psum(1, mesh_name)
+        leaves = [(kk, (kk + 1) % sides) for kk in range(sides)]
+        all_rows = [(w, ii) for ii, w in leaves]
+        even, seen_now = ([], [])
+        for to_i in range(sides - 1):
+            if to_i % 2 == 0:
+                even.append(lax.ppermute(even[-1] if even else content, mesh_name, leaves))
+            else:
+                earlier = lax.ppermute(seen_now[-1] if seen_now else content, mesh_name, all_rows)
+                seen_now.append(earlier)
+        x_new = jnp.stack([*even[::-1], content, *seen_now], axis=0)
+        v_now = lax.axis_index(mesh_name) - len(even)
+        x_new = x_new[(jnp.arange(sides) - v_now) % sides]
+        return bind_the_records(x_new, where_dim)
+
     data_index = lax.axis_index("dp")
     head_index = lax.axis_index("tensor")
     weight_rows = wq_codes.shape[0]
@@ -75,7 +98,7 @@
     length = sequence.shape[0]
     full_q, full_k, full_v = (
         lax.all_gather(wq_local, "dp", axis=0, tiled=True),
-        lax.all_gather(wk_used, "dp", axis=0, tiled=True),
+        replace_cards_all("dp", 0, wk_used),
         lax.all_gather(wv_used, "dp", axis=0, tiled=True),
     )
     query_lin = jnp.dot(sequence, full_q, preferred_element_type=jnp.float32)

time: 299 us -> 258 us (0.86)
  waiting for transfers between devices: 250 us -> 179 us
  starting transfers between devices: 5.3 us -> 36.8 us
    all_gather x1, waiting for transfers between devices: 46 us -> 0.02 us  [body(): sequence = lax.all_gather(tokens, 'tensor', axis=0, tiled=True)]
    ppermute x0 -> x15, starting transfers between devices: none -> 31.5 us  [the longest x7 31.4 us: replace_cards_all(): lax.ppermute(seen_now[-1] if seen_now else content, mesh_name, all_rows)]
    all_gather x1 -> x0, waiting for transfers between devices: 28.1 us -> none  [body(): lax.all_gather(wk_used, 'dp', axis=0, tiled=True)]
    ppermute x0 -> x15, waiting for transfers between devices: none -> 21.8 us  [the longest x8 17.8 us: replace_cards_all(): even.append(lax.ppermute(even[-1] if even else content, mesh_name, leaves))]
    all_gather x1, waiting for transfers between devices: 48.3 us -> 27.4 us  [body(): lax.all_gather(wq_local, 'dp', axis=0, tiled=True)]
  transfers between devices with their start and end apart: 8 -> 22, of which waited for: 8 -> 18; matrix products, arithmetic and copies ran while one was open for 7% -> 9% of each run, Pallas kernels for 0% -> 0%
where the time goes in v1:
time: 258 us
  waiting for transfers between devices  179 us (69%)
  starting transfers between devices  36.8 us (14%)
  matrix products  23.9 us (9%)
  between operations  13.4 us (5%)
  other arithmetic  3.26 us (1%)
    all_gather x1, waiting for transfers between devices, body(): wo_whole = lax.all_gather(wo_local, 'dp', axis=1, tiled=True)  50.1 us
    reduce_scatter x1, waiting for transfers between devices, body(): lax.psum_scatter(terms.astype(jnp.bfloat16), 'tensor', scatter_dimension=...  41.7 us
    ppermute x7, starting transfers between devices, replace_cards_all(): lax.ppermute(seen_now[-1] if seen_now else content, mesh_name, all_rows)  31.4 us
    all_gather x1, waiting for transfers between devices, body(): lax.all_gather(wv_used, 'dp', axis=0, tiled=True)  31 us
    all_gather x1, waiting for transfers between devices, body(): lax.all_gather(wq_local, 'dp', axis=0, tiled=True)  27.4 us
    ppermute x8, waiting for transfers between devices, replace_cards_all(): even.append(lax.ppermute(even[-1] if even else content, mesh_name, leaves))  17.8 us
    ppermute x2, waiting for transfers between devices, from_partner(): return lax.ppermute(value, axis, pairs)  5.81 us
    dot_general x1, matrix products, body(): terms = jnp.dot(attended, wo_whole, preferred_element_type=jnp.float32)  5.69 us
  transfers between devices with their start and end apart: 22, of which 18 were waited for; matrix products, arithmetic and copies ran while one was open for 9% of the time, Pallas kernels for 0%

profile of v1, /device:TPU:0, one launch (start us, length us, event | category | flops | bytes accessed | tf_op | source)
XLA Modules:
  0.0 257.7 jit_solution(8792375805459228327)
XLA Ops:
  8.3 2.2 fusion.2
  11.4 3.0 %collective-permute-start = (bf16[256,64]{1,0:T(8,128)(2,1)S(1)}, bf16[256,64]{1,0:T(8,128)(2,1)S(1)}, u32[]{:S(2)}, u32[]{:S(2)}) collective-permute-start(bf16[256,64]{1,0:T(8,128)(2,1)S(1)} %get-tuple-element.13), channel_id=1, source_target_pairs={{0,1},{1,0},{2,3},{3,2},{4,5},{5,4},{6,7},{7,6},{8,9},{9,8},{10,11... | collective-permute-start | bytes 98312 | tf_op jit(solution)/shard_map/ppermute | solution.py:22
  14.4 2.2 collective-permute-done
  19.1 2.1 collective-permute-start.1
  21.2 3.6 %collective-permute-done.1 = bf16[256,64]{1,0:T(8,128)(2,1)S(1)} collective-permute-done((bf16[256,64]{1,0:T(8,128)(2,1)S(1)}, bf16[256,64]{1,0:T(8,128)(2,1)S(1)}, u32[]{:S(2)}, u32[]{:S(2)}) %collective-permute-start.1) | collective-permute-done | bytes 32800 | tf_op jit(solution)/shard_map/ppermute | solution.py:22
  24.9 6.4 %collective-permute-done.2 = bf16[256,128]{1,0:T(8,128)(2,1)S(1)} collective-permute-done((bf16[256,128]{1,0:T(8,128)(2,1)S(1)}, bf16[256,128]{1,0:T(8,128)(2,1)S(1)}, u32[]{:S(2)}, u32[]{:S(2)}) %collective-permute-start.2) | collective-permute-done | bytes 65568 | tf_op jit(solution)/shard_map/ppermute | solution.py:71
  31.3 4.4 %collective-permute-start.10 = (bf16[256,128]{1,0:T(8,128)(2,1)S(1)}, bf16[256,128]{1,0:T(8,128)(2,1)S(1)}, u32[]{:S(2)}, u32[]{:S(2)}) collective-permute-start(bf16[256,128]{1,0:T(8,128)(2,1)S(1)} %maximum_select_fusion.1), channel_id=1, source_target_pairs={{2,0},{4,2},{6,4},{8,6},{10,8},{12,10},{14,12},{16,14},{18,16},{20... | collective-permute-start | bytes 196616 | tf_op jit(solution)/shard_map/ppermute | solution.py:73
  35.8 1.9 collective-permute-done.3
  37.7 4.4 %collective-permute-start.11 = (bf16[256,128]{1,0:T(8,128)(2,1)S(1)}, bf16[256,128]{1,0:T(8,128)(2,1)S(1)}, u32[]{:S(2)}, u32[]{:S(2)}) collective-permute-start(bf16[256,128]{1,0:T(8,128)(2,1)S(1)} %collective-permute-done.10), channel_id=1, source_target_pairs={{2,0},{4,2},{6,4},{8,6},{10,8},{12,10},{14,12},{16,14},{18,16},{20... | collective-permute-start | bytes 196616 | tf_op jit(solution)/shard_map/ppermute | solution.py:73
  42.2 1.9 collective-permute-done.4
  44.1 4.5 %collective-permute-start.12 = (bf16[256,128]{1,0:T(8,128)(2,1)S(1)}, bf16[256,128]{1,0:T(8,128)(2,1)S(1)}, u32[]{:S(2)}, u32[]{:S(2)}) collective-permute-start(bf16[256,128]{1,0:T(8,128)(2,1)S(1)} %collective-permute-done.11), channel_id=1, source_target_pairs={{2,0},{4,2},{6,4},{8,6},{10,8},{12,10},{14,12},{16,14},{18,16},{20... | collective-permute-start | bytes 196616 | tf_op jit(solution)/shard_map/ppermute | solution.py:73
  48.6 2.0 collective-permute-done.5
  51.4 4.5 %collective-permute-start.13 = (bf16[256,128]{1,0:T(8,128)(2,1)S(1)}, bf16[256,128]{1,0:T(8,128)(2,1)S(1)}, u32[]{:S(2)}, u32[]{:S(2)}) collective-permute-start(bf16[256,128]{1,0:T(8,128)(2,1)S(1)} %collective-permute-done.12), channel_id=1, source_target_pairs={{2,0},{4,2},{6,4},{8,6},{10,8},{12,10},{14,12},{16,14},{18,16},{20... | collective-permute-start | bytes 196616 | tf_op jit(solution)/shard_map/ppermute | solution.py:73
  57.8 4.5 %collective-permute-start.14 = (bf16[256,128]{1,0:T(8,128)(2,1)S(1)}, bf16[256,128]{1,0:T(8,128)(2,1)S(1)}, u32[]{:S(2)}, u32[]{:S(2)}) collective-permute-start(bf16[256,128]{1,0:T(8,128)(2,1)S(1)} %collective-permute-done.13), channel_id=1, source_target_pairs={{2,0},{4,2},{6,4},{8,6},{10,8},{12,10},{14,12},{16,14},{18,16},{20... | collective-permute-start | bytes 196616 | tf_op jit(solution)/shard_map/ppermute | solution.py:73
  64.2 4.5 %collective-permute-start.15 = (bf16[256,128]{1,0:T(8,128)(2,1)S(1)}, bf16[256,128]{1,0:T(8,128)(2,1)S(1)}, u32[]{:S(2)}, u32[]{:S(2)}) collective-permute-start(bf16[256,128]{1,0:T(8,128)(2,1)S(1)} %collective-permute-done.14), channel_id=1, source_target_pairs={{2,0},{4,2},{6,4},{8,6},{10,8},{12,10},{14,12},{16,14},{18,16},{20... | collective-permute-start | bytes 196616 | tf_op jit(solution)/shard_map/ppermute | solution.py:73
  71.6 4.6 %collective-permute-start.16 = (bf16[256,128]{1,0:T(8,128)(2,1)S(1)}, bf16[256,128]{1,0:T(8,128)(2,1)S(1)}, u32[]{:S(2)}, u32[]{:S(2)}) collective-permute-start(bf16[256,128]{1,0:T(8,128)(2,1)S(1)} %collective-permute-done.15), channel_id=1, source_target_pairs={{2,0},{4,2},{6,4},{8,6},{10,8},{12,10},{14,12},{16,14},{18,16},{20... | collective-permute-start | bytes 196616 | tf_op jit(solution)/shard_map/ppermute | solution.py:73
  80.2 3.0 %convolution_bitcast_fusion = f32[384,1,128]{0,2,1:T(8,128)S(1)} fusion(bf16[4096,128]{1,0:T(8,128)(2,1)S(1)} %bitcast.92, bf16[384,4096]{1,0:T(8,128)(2,1)} %all-gather.7.cloned.1.call-done), kind=kOutput, calls=%fused_computation.13 | convolution fusion | flops 402653184 | bytes 4390912 | tf_op jit(solution)/shard_map/dot_general | solution.py:105
  83.7 27.4 %all-gather.9.cloned.1.call-done = bf16[4096,512]{1,0:T(8,128)(2,1)} async-done(((bf16[256,512]{1,0:T(8,128)(2,1)}), bf16[4096,512]{1,0:T(8,128)(2,1)}) %all-gather.9.cloned.1.call-update) | async-done | bytes 4194320 | tf_op jit(solution)/shard_map/all_gather | solution.py:100
  111.0 5.5 %fusion.40 = f32[512,384]{1,0:T(8,128)S(1)} fusion(bf16[4096,512]{1,0:T(8,128)(2,1)} %all-gather.9.cloned.1.call-done, bf16[384,4096]{1,0:T(8,128)(2,1)} %all-gather.7.cloned.1.call-done), kind=kOutput, calls=%fused_computation.104 | convolution fusion | flops 1610612736 | bytes 8126464 | tf_op jit(solution)/shard_map/dot_general | solution.py:104
  118.6 31.0 %all-gather.5.cloned.1.call-done = bf16[4096,128]{1,0:T(8,128)(2,1)} async-done(((bf16[256,128]{1,0:T(8,128)(2,1)}), bf16[4096,128]{1,0:T(8,128)(2,1)}) %all-gather.5.cloned.1.call-update) | async-done | bytes 1048592 | tf_op jit(solution)/shard_map/all_gather | solution.py:102
  149.7 4.1 %convolution_convert_fusion.1 = bf16[128,4,384]{2,0,1:T(8,128)(2,1)S(1)} fusion(f32[384,384,4]{1,0,2:T(8,128)S(1)} %get-tuple-element.16, f32[4,384]{1,0:T(4,128)S(1)} %fusion, f32[4,384]{1,0:T(4,128)S(1)} %get-tuple-element.15, pred[384,384]{0,1:T(8,128)(4,1)S(1)} %iota_compare_fusion, bf16[4096,128]{1,0:T(8,128)(2,1)} %all-gather.5.cloned.1.call-done, ...), kind=kOutput, calls=%fused_computation.7 | convolution fusion | flops 556843008 | bytes 7106560 | tf_op jit(solution)/shard_map/chqk,ckd->cqhd/dot_general | solution.py:126
  153.7 50.1 %all-gather.11.cloned.1.call-done = bf16[512,4096]{1,0:T(8,128)(2,1)} async-done(((bf16[512,256]{1,0:T(8,128)(2,1)}), bf16[512,4096]{1,0:T(8,128)(2,1)}) %all-gather.11.cloned.1.call-update) | async-done | bytes 4194320 | tf_op jit(solution)/shard_map/all_gather | solution.py:92
  203.8 5.7 %convolution_convert_fusion = bf16[384,4096]{1,0:T(8,128)(2,1)} fusion(bf16[384,512]{0,1:T(8,128)(2,1)S(1)} %bitcast.95, bf16[512,4096]{1,0:T(8,128)(2,1)} %all-gather.11.cloned.1.call-done), kind=kOutput, calls=%fused_computation.1 | convolution fusion | flops 1612185600 | bytes 7733248 | tf_op jit(solution)/shard_map/dot_general | solution.py:130
  209.5 41.7 %reduce-scatter.2.cloned.1.call-done = bf16[192,4096]{1,0:T(8,128)(2,1)} async-done(((bf16[384,4096]{1,0:T(8,128)(2,1)}), bf16[192,4096]{1,0:T(8,128)(2,1)}) %reduce-scatter.2.cloned.1.call-update) | async-done | bytes 1572880 | tf_op jit(solution)/shard_map/reduce_scatter | solution.py:131
  (85 shorter events, 19.2 us)
Async XLA Ops:
  6.5 11.0 %copy-start = (f32[8,32]{1,0:T(8,128)S(1)}, f32[8,32]{1,0:T(8,128)}, u32[]{:S(2)}) copy-start(f32[8,32]{1,0:T(8,128)} %param.17) | copy-start | bytes 3076
  6.5 11.3 %copy-start.1 = (bf16[512,256]{1,0:T(8,128)(2,1)S(1)}, bf16[512,256]{1,0:T(8,128)(2,1)}, u32[]{:S(2)}) copy-start(bf16[512,256]{1,0:T(8,128)(2,1)} %param.16) | copy-start | bytes 786436
  6.6 73.7 %all-gather.7.cloned.1.call-start = ((), (), s32[]{:S(2)}) async-start(), calls=%async_computation.2 | async-start | bytes 4718592 | tf_op jit(solution)/shard_map/all_gather | solution.py:93
  7.3 103.7 %all-gather.9.cloned.1.call-start = ((), (), s32[]{:S(2)}) async-start(), calls=%async_computation.3 | async-start | bytes 4456448 | tf_op jit(solution)/shard_map/all_gather | solution.py:100
  10.4 139.2 %all-gather.5.cloned.1.call-start = ((), (), s32[]{:S(2)}) async-start(), calls=%async_computation.1 | async-start | bytes 1114112 | tf_op jit(solution)/shard_map/all_gather | solution.py:102
  11.4 5.2 %collective-permute-start = (bf16[256,64]{1,0:T(8,128)(2,1)S(1)}, bf16[256,64]{1,0:T(8,128)(2,1)S(1)}, u32[]{:S(2)}, u32[]{:S(2)}) collective-permute-start(bf16[256,64]{1,0:T(8,128)(2,1)S(1)} %get-tuple-element.13), channel_id=1, source_target_pairs={{0,1},{1,0},{2,3},{3,2},{4,5},{5,4},{6,7},{7,6},{8,9},{9,8},{10,11... | collective-permute-start | bytes 98312 | tf_op jit(solution)/shard_map/ppermute | solution.py:22
  17.4 186.4 %all-gather.11.cloned.1.call-start = ((), (), s32[]{:S(2)}) async-start(), calls=%async_computation.4 | async-start | bytes 4456448 | tf_op jit(solution)/shard_map/all_gather | solution.py:92
  19.1 232.1 %reduce-scatter.2.cloned.1.call-start = ((), (), s32[]{:S(2)}) async-start(), calls=%async_computation.5 | async-start | bytes 4718592 | tf_op jit(solution)/shard_map/reduce_scatter | solution.py:131
  19.1 5.7 %collective-permute-start.1 = (bf16[256,64]{1,0:T(8,128)(2,1)S(1)}, bf16[256,64]{1,0:T(8,128)(2,1)S(1)}, u32[]{:S(2)}, u32[]{:S(2)}) collective-permute-start(bf16[256,64]{1,0:T(8,128)(2,1)S(1)} %get-tuple-element.14), channel_id=1, source_target_pairs={{0,1},{1,0},{2,3},{3,2},{4,5},{5,4},{6,7},{7,6},{8,9},{9,8},{10,11... | collective-permute-start | bytes 98312 | tf_op jit(solution)/shard_map/ppermute | solution.py:22
  24.9 6.4 %collective-permute-start.2 = (bf16[256,128]{1,0:T(8,128)(2,1)S(1)}, bf16[256,128]{1,0:T(8,128)(2,1)S(1)}, u32[]{:S(2)}, u32[]{:S(2)}) collective-permute-start(bf16[256,128]{1,0:T(8,128)(2,1)S(1)} %maximum_select_fusion.1), channel_id=1, source_target_pairs={{0,2},{2,4},{4,6},{6,8},{8,10},{10,12},{12,14},{14,16},{16,18},{18... | collective-permute-start | bytes 196616 | tf_op jit(solution)/shard_map/ppermute | solution.py:71
  31.3 6.4 %collective-permute-start.3 = (bf16[256,128]{1,0:T(8,128)(2,1)S(1)}, bf16[256,128]{1,0:T(8,128)(2,1)S(1)}, u32[]{:S(2)}, u32[]{:S(2)}) collective-permute-start(bf16[256,128]{1,0:T(8,128)(2,1)S(1)} %collective-permute-done.2), channel_id=1, source_target_pairs={{0,2},{2,4},{4,6},{6,8},{8,10},{10,12},{12,14},{14,16},{16,18},{18... | collective-permute-start | bytes 196616 | tf_op jit(solution)/shard_map/ppermute | solution.py:71
  31.3 6.4 %collective-permute-start.10 = (bf16[256,128]{1,0:T(8,128)(2,1)S(1)}, bf16[256,128]{1,0:T(8,128)(2,1)S(1)}, u32[]{:S(2)}, u32[]{:S(2)}) collective-permute-start(bf16[256,128]{1,0:T(8,128)(2,1)S(1)} %maximum_select_fusion.1), channel_id=1, source_target_pairs={{2,0},{4,2},{6,4},{8,6},{10,8},{12,10},{14,12},{16,14},{18,16},{20... | collective-permute-start | bytes 196616 | tf_op jit(solution)/shard_map/ppermute | solution.py:73
  37.7 6.4 %collective-permute-start.4 = (bf16[256,128]{1,0:T(8,128)(2,1)S(1)}, bf16[256,128]{1,0:T(8,128)(2,1)S(1)}, u32[]{:S(2)}, u32[]{:S(2)}) collective-permute-start(bf16[256,128]{1,0:T(8,128)(2,1)S(1)} %collective-permute-done.3), channel_id=1, source_target_pairs={{0,2},{2,4},{4,6},{6,8},{8,10},{10,12},{12,14},{14,16},{16,18},{18... | collective-permute-start | bytes 196616 | tf_op jit(solution)/shard_map/ppermute | solution.py:71
  37.7 6.4 %collective-permute-start.11 = (bf16[256,128]{1,0:T(8,128)(2,1)S(1)}, bf16[256,128]{1,0:T(8,128)(2,1)S(1)}, u32[]{:S(2)}, u32[]{:S(2)}) collective-permute-start(bf16[256,128]{1,0:T(8,128)(2,1)S(1)} %collective-permute-done.10), channel_id=1, source_target_pairs={{2,0},{4,2},{6,4},{8,6},{10,8},{12,10},{14,12},{16,14},{18,16},{20... | collective-permute-start | bytes 196616 | tf_op jit(solution)/shard_map/ppermute | solution.py:73
  44.1 6.5 %collective-permute-start.5 = (bf16[256,128]{1,0:T(8,128)(2,1)S(1)}, bf16[256,128]{1,0:T(8,128)(2,1)S(1)}, u32[]{:S(2)}, u32[]{:S(2)}) collective-permute-start(bf16[256,128]{1,0:T(8,128)(2,1)S(1)} %collective-permute-done.4), channel_id=1, source_target_pairs={{0,2},{2,4},{4,6},{6,8},{8,10},{10,12},{12,14},{14,16},{16,18},{18... | collective-permute-start | bytes 196616 | tf_op jit(solution)/shard_map/ppermute | solution.py:71
  44.1 7.2 %collective-permute-start.12 = (bf16[256,128]{1,0:T(8,128)(2,1)S(1)}, bf16[256,128]{1,0:T(8,128)(2,1)S(1)}, u32[]{:S(2)}, u32[]{:S(2)}) collective-permute-start(bf16[256,128]{1,0:T(8,128)(2,1)S(1)} %collective-permute-done.11), channel_id=1, source_target_pairs={{2,0},{4,2},{6,4},{8,6},{10,8},{12,10},{14,12},{16,14},{18,16},{20... | collective-permute-start | bytes 196616 | tf_op jit(solution)/shard_map/ppermute | solution.py:73
  50.6 6.5 %collective-permute-start.6 = (bf16[256,128]{1,0:T(8,128)(2,1)S(1)}, bf16[256,128]{1,0:T(8,128)(2,1)S(1)}, u32[]{:S(2)}, u32[]{:S(2)}) collective-permute-start(bf16[256,128]{1,0:T(8,128)(2,1)S(1)} %collective-permute-done.5), channel_id=1, source_target_pairs={{0,2},{2,4},{4,6},{6,8},{8,10},{10,12},{12,14},{14,16},{16,18},{18... | collective-permute-start | bytes 196616 | tf_op jit(solution)/shard_map/ppermute | solution.py:71
  51.4 6.4 %collective-permute-start.13 = (bf16[256,128]{1,0:T(8,128)(2,1)S(1)}, bf16[256,128]{1,0:T(8,128)(2,1)S(1)}, u32[]{:S(2)}, u32[]{:S(2)}) collective-permute-start(bf16[256,128]{1,0:T(8,128)(2,1)S(1)} %collective-permute-done.12), channel_id=1, source_target_pairs={{2,0},{4,2},{6,4},{8,6},{10,8},{12,10},{14,12},{16,14},{18,16},{20... | collective-permute-start | bytes 196616 | tf_op jit(solution)/shard_map/ppermute | solution.py:73
  57.1 6.5 %collective-permute-start.7 = (bf16[256,128]{1,0:T(8,128)(2,1)S(1)}, bf16[256,128]{1,0:T(8,128)(2,1)S(1)}, u32[]{:S(2)}, u32[]{:S(2)}) collective-permute-start(bf16[256,128]{1,0:T(8,128)(2,1)S(1)} %collective-permute-done.6), channel_id=1, source_target_pairs={{0,2},{2,4},{4,6},{6,8},{8,10},{10,12},{12,14},{14,16},{16,18},{18... | collective-permute-start | bytes 196616 | tf_op jit(solution)/shard_map/ppermute | solution.py:71
  57.8 6.4 %collective-permute-start.14 = (bf16[256,128]{1,0:T(8,128)(2,1)S(1)}, bf16[256,128]{1,0:T(8,128)(2,1)S(1)}, u32[]{:S(2)}, u32[]{:S(2)}) collective-permute-start(bf16[256,128]{1,0:T(8,128)(2,1)S(1)} %collective-permute-done.13), channel_id=1, source_target_pairs={{2,0},{4,2},{6,4},{8,6},{10,8},{12,10},{14,12},{16,14},{18,16},{20... | collective-permute-start | bytes 196616 | tf_op jit(solution)/shard_map/ppermute | solution.py:73
  63.6 6.5 %collective-permute-start.8 = (bf16[256,128]{1,0:T(8,128)(2,1)S(1)}, bf16[256,128]{1,0:T(8,128)(2,1)S(1)}, u32[]{:S(2)}, u32[]{:S(2)}) collective-permute-start(bf16[256,128]{1,0:T(8,128)(2,1)S(1)} %collective-permute-done.7), channel_id=1, source_target_pairs={{0,2},{2,4},{4,6},{6,8},{8,10},{10,12},{12,14},{14,16},{16,18},{18... | collective-permute-start | bytes 196616 | tf_op jit(solution)/shard_map/ppermute | solution.py:71
  64.2 7.5 %collective-permute-start.15 = (bf16[256,128]{1,0:T(8,128)(2,1)S(1)}, bf16[256,128]{1,0:T(8,128)(2,1)S(1)}, u32[]{:S(2)}, u32[]{:S(2)}) collective-permute-start(bf16[256,128]{1,0:T(8,128)(2,1)S(1)} %collective-permute-done.14), channel_id=1, source_target_pairs={{2,0},{4,2},{6,4},{8,6},{10,8},{12,10},{14,12},{16,14},{18,16},{20... | collective-permute-start | bytes 196616 | tf_op jit(solution)/shard_map/ppermute | solution.py:73
  70.1 7.8 %collective-permute-start.9 = (bf16[256,128]{1,0:T(8,128)(2,1)S(1)}, bf16[256,128]{1,0:T(8,128)(2,1)S(1)}, u32[]{:S(2)}, u32[]{:S(2)}) collective-permute-start(bf16[256,128]{1,0:T(8,128)(2,1)S(1)} %collective-permute-done.8), channel_id=1, source_target_pairs={{0,2},{2,4},{4,6},{6,8},{8,10},{10,12},{12,14},{14,16},{16,18},{18... | collective-permute-start | bytes 196616 | tf_op jit(solution)/shard_map/ppermute | solution.py:71
  71.6 7.8 %collective-permute-start.16 = (bf16[256,128]{1,0:T(8,128)(2,1)S(1)}, bf16[256,128]{1,0:T(8,128)(2,1)S(1)}, u32[]{:S(2)}, u32[]{:S(2)}) collective-permute-start(bf16[256,128]{1,0:T(8,128)(2,1)S(1)} %collective-permute-done.15), channel_id=1, source_target_pairs={{2,0},{4,2},{6,4},{8,6},{10,8},{12,10},{14,12},{16,14},{18,16},{20... | collective-permute-start | bytes 196616 | tf_op jit(solution)/shard_map/ppermute | solution.py:73
  (4 other events, 16.7 us)
Sparse Core Ops, SparseCore 0:
  8.9 48.3 all-gather.6
  59.5 51.4 all-gather.8
  113.2 36.4 all-gather.4
  151.7 52.1 all-gather.10
  209.7 41.4 reduce-scatter.1
